TPU v7x, 128 devices: a whole 4x4x4 slice. The times are simulated.
128 devices in a mesh: depth: 8 (over z, y_lo), height: 16 (over x, y_hi, core).
Axes of the slice: x: 4, y: 4 (y_hi: 2, y_lo: 2; y = y_hi * 2 + y_lo), z: 4, core: 2. Of those that a mesh axis runs over, the one named last changes fastest.
Arguments:
- volume: bfloat16 [32, 32, 128, 128], P(None, 'depth', 'height'), may hold values from -6 to 6
- filters_three: bfloat16 [27, 64, 32], replicated, may hold values from -0.21875 to 0.21875
- filters_four: bfloat16 [27, 128, 64], P(None, 'height'), may hold values from -0.15625 to 0.15625
- cotangent: bfloat16 [128, 16, 64, 64], P(None, 'depth', 'height'), may hold values from -6 to 6
Outputs:
- grad_volume: bfloat16 [32, 32, 128, 128], P(None, 'depth', 'height')
- grad_three: float32 [27, 64, 32], replicated
- grad_four: float32 [27, 128, 64], P(None, 'height')
All inputs are finite; a program needn't handle non-finite values.
Results may differ from a plain program's by a relative error of at most 0.023.
Values may be sent and summed in bfloat16 or wider, within the bound.
A program may use at most 256 MiB of HBM per device.

v0:
```python
import math
import jax
import jax.numpy as jnp
from jax import lax
from jax.sharding import PartitionSpec as P

TANH_SCALE = 0.7978845608028654
CUBIC_TERM = 0.044715


def extended_2(x, sides, width):
    for axis, dim in sides:
        size, length = (lax.axis_size(axis), x.shape[dim])
        up = [(i, (i + 1) % size) for i in range(size - 1)]
        down = [(j, i) for i, j in up]
        last = lax.slice_in_dim(x, length - width, length, axis=dim)
        first = lax.slice_in_dim(x, 0, width, axis=dim)
        before = lax.ppermute(last, axis, up)
        after = lax.ppermute(first, axis, down)
        x = jnp.concatenate([before, x, after], axis=dim)
    return x


def gelu_value(values_in):
    inner = jnp.tanh(TANH_SCALE * (values_in + CUBIC_TERM * values_in * values_in * values_in))
    return 0.5 * values_in * (1.0 + inner)


def gelu_slope(values_in):
    inner = jnp.tanh(TANH_SCALE * (values_in + CUBIC_TERM * values_in * values_in * values_in))
    return 0.5 * (1.0 + inner) + 0.5 * values_in * (1.0 - inner * inner) * TANH_SCALE * (
        1.0 + 3.0 * CUBIC_TERM * values_in * values_in
    )


def pad_width(values_in):
    return jnp.pad(values_in, ((0, 0), (0, 0), (0, 0), (1, 1)))


def forward_taps(padded, weights, depth_cells, height_cells, width_cells):
    running = jnp.zeros((weights.shape[1], depth_cells, height_cells, width_cells), jnp.float32)
    for first in range(3):
        for second in range(3):
            for third in range(3):
                window_piece = padded[
                    :,
                    first : first + depth_cells,
                    second : second + height_cells,
                    third : third + width_cells,
                ]
                running = running + jnp.einsum(
                    "oi,idhw->odhw",
                    weights[9 * first + 3 * second + third],
                    window_piece,
                    preferred_element_type=jnp.float32,
                )
    return running


def transpose_taps(padded, weights, depth_cells, height_cells, width_cells):
    running = jnp.zeros((weights.shape[2], depth_cells, height_cells, width_cells), jnp.float32)
    for first in range(3):
        for second in range(3):
            for third in range(3):
                window_piece = padded[
                    :,
                    2 - first : 2 - first + depth_cells,
                    2 - second : 2 - second + height_cells,
                    2 - third : 2 - third + width_cells,
                ]
                running = running + jnp.einsum(
                    "oi,odhw->idhw",
                    weights[9 * first + 3 * second + third],
                    window_piece,
                    preferred_element_type=jnp.float32,
                )
    return running


def weight_taps(delta, padded, depth_cells, height_cells, width_cells):
    collected = []
    for first in range(3):
        for second in range(3):
            for third in range(3):
                window_piece = padded[
                    :,
                    first : first + depth_cells,
                    second : second + height_cells,
                    third : third + width_cells,
                ]
                collected.append(
                    jnp.einsum(
                        "odhw,idhw->oi", delta, window_piece, preferred_element_type=jnp.float32
                    )
                )
    return jnp.stack(collected, axis=0)


def shards(volume, filters_three, filters_four, cotangent):
    channels_in, depth_cells, height_cells, width_cells = volume.shape
    depth_count = lax.axis_size("depth")
    height_count = lax.axis_size("height")
    scale_three = 1.0 / math.sqrt(
        depth_cells * depth_count * height_cells * height_count * width_cells
    )
    scale_four = 1.0 / math.sqrt(
        depth_cells * depth_count // 2 * (height_cells * height_count // 2) * (width_cells // 2)
    )
    half_depth = depth_cells // 2
    half_height = height_cells // 2
    half_width = width_cells // 2
    extended = extended_2(volume, (("depth", 1), ("height", 2)), 1)
    padded = pad_width(extended)
    act_three = forward_taps(padded, filters_three, depth_cells, height_cells, width_cells)
    channels_mid = act_three.shape[0]
    hidden = gelu_value(act_three).reshape(
        channels_mid, half_depth, 2, half_height, 2, half_width, 2
    )
    pooled = (jnp.sum(hidden, axis=(2, 4, 6)) * 0.125).astype(jnp.bfloat16)
    full_bank = lax.all_gather(filters_four, "height", axis=1, tiled=True)
    rimmed = extended_2(pooled, (("depth", 1), ("height", 2)), 1)
    pooled_pad = pad_width(rimmed)
    act_four = forward_taps(pooled_pad, full_bank, half_depth, half_height, half_width)
    delta_four = (cotangent.astype(jnp.float32) * gelu_slope(act_four)).astype(jnp.bfloat16)
    partial_four = weight_taps(delta_four, pooled_pad, half_depth, half_height, half_width)
    depth_summed = lax.psum(partial_four.astype(jnp.bfloat16), "depth")
    grad_four = (
        lax.psum_scatter(depth_summed, "height", scatter_dimension=1, tiled=True).astype(
            jnp.float32
        )
        * scale_four
    )
    delta_rim = extended_2(delta_four, (("depth", 1), ("height", 2)), 1)
    back_pooled = transpose_taps(
        pad_width(delta_rim), full_bank, half_depth, half_height, half_width
    )
    spread = (
        jnp.repeat(jnp.repeat(jnp.repeat(back_pooled, 2, axis=1), 2, axis=2), 2, axis=3) * 0.125
    )
    delta_three = (spread * gelu_slope(act_three)).astype(jnp.bfloat16)
    partial_three = weight_taps(delta_three, padded, depth_cells, height_cells, width_cells)
    grad_three = lax.psum(partial_three, ("depth", "height")) * scale_three
    delta_extended = extended_2(delta_three, (("depth", 1), ("height", 2)), 1)
    grad_volume = transpose_taps(
        pad_width(delta_extended), filters_three, depth_cells, height_cells, width_cells
    ).astype(jnp.bfloat16)
    return (grad_volume, grad_three, grad_four)


def solution(mesh):
    in_specs = (
        P(None, "depth", "height", None),
        P(),
        P(None, "height", None),
        P(None, "depth", "height", None),
    )
    out_specs = (P(None, "depth", "height", None), P(), P(None, "height", None))
    return jax.shard_map(shards, mesh=mesh, in_specs=in_specs, out_specs=out_specs, check_vma=False)
```

profile of v0, /device:TPU:6, one launch (start us, length us, event | category | flops | bytes accessed | tf_op | source)
XLA Modules:
  0.0 348.1 jit_solution(2866375884435285282)
XLA Ops:
  9.0 3.5 %collective-permute-start = (bf16[32,1,8,128]{3,0,2,1:T(8,128)(2,1)S(1)}, bf16[32,1,8,128]{3,0,2,1:T(8,128)(2,1)S(1)}, u32[]{:S(2)}, u32[]{:S(2)}) collective-permute-start(bf16[32,1,8,128]{3,0,2,1:T(8,128)(2,1)S(1)} %copy.321), channel_id=1, source_target_pairs={{0,16},{16,32},{32,48},{48,64},{64,80},{80,96},{96,112},{1,17},{17... | collective-permute-start | bytes 196616 | tf_op jit(solution)/shard_map/ppermute | solution.py:18
  15.6 3.1 collective-permute-done.1
  18.8 1.9 collective-permute-start.2
  20.7 6.0 %collective-permute-start.3 = (bf16[32,6,1,128]{3,0,2,1:T(8,128)(2,1)S(1)}, bf16[32,6,1,128]{3,0,2,1:T(8,128)(2,1)S(1)}, u32[]{:S(2)}, u32[]{:S(2)}) collective-permute-start(bf16[32,6,1,128]{3,0,2,1:T(8,128)(2,1)S(1)} %get-tuple-element.19), channel_id=1, source_target_pairs={{1,0},{2,1},{3,2},{4,3},{5,4},{6,5},{7,6},{8,7},{9,8},{10,9},{11,1... | collective-permute-start | bytes 147464 | tf_op jit(solution)/shard_map/ppermute | solution.py:19
  38.3 2.0 add_multiply_fusion
  40.4 1.8 copy.91
  42.2 2.4 reduce_sum.9
  45.6 4.6 %collective-permute-start.4 = (bf16[64,1,4,64]{0,3,2,1:T(8,128)(2,1)S(1)}, bf16[64,1,4,64]{0,3,2,1:T(8,128)(2,1)S(1)}, u32[]{:S(2)}, u32[]{:S(2)}) collective-permute-start(bf16[64,1,4,64]{0,3,2,1:T(8,128)(2,1)S(1)} %get-tuple-element.33), channel_id=1, source_target_pairs={{0,16},{16,32},{32,48},{48,64},{64,80},{80,96},{96,112},{1,17},{17... | collective-permute-start | bytes 98312 | tf_op jit(solution)/shard_map/ppermute | solution.py:18
  51.5 23.7 %all_gather.3 = bf16[27,128,64]{2,1,0:T(8,128)(2,1)S(1)} all-gather(bf16[27,8,64]{2,1,0:T(8,128)(2,1)S(1)} %copy-done.14), channel_id=1, replica_groups=mesh['depth'=8,'height'=16] {'height'}, dimensions={1}, use_global_device_ids=true | all-gather | bytes 470016 | tf_op jit(solution)/shard_map/all_gather | solution.py:120
  75.2 2.3 collective-permute-start.6
  77.5 5.7 %collective-permute-start.7 = (bf16[64,4,1,64]{0,3,2,1:T(8,128)(2,1)S(1)}, bf16[64,4,1,64]{0,3,2,1:T(8,128)(2,1)S(1)}, u32[]{:S(2)}, u32[]{:S(2)}) collective-permute-start(bf16[64,4,1,64]{0,3,2,1:T(8,128)(2,1)S(1)} %get-tuple-element.25), channel_id=1, source_target_pairs={{1,0},{2,1},{3,2},{4,3},{5,4},{6,5},{7,6},{8,7},{9,8},{10,9},{11,1... | collective-permute-start | bytes 98312 | tf_op jit(solution)/shard_map/ppermute | solution.py:19
  96.6 4.0 %collective-permute-start.8 = (bf16[128,1,4,64]{0,3,2,1:T(8,128)(2,1)S(1)}, bf16[128,1,4,64]{0,3,2,1:T(8,128)(2,1)S(1)}, u32[]{:S(2)}, u32[]{:S(2)}) collective-permute-start(bf16[128,1,4,64]{0,3,2,1:T(8,128)(2,1)S(1)} %get-tuple-element.31), channel_id=1, source_target_pairs={{0,16},{16,32},{32,48},{48,64},{64,80},{80,96},{96,112},{1,17},{17... | collective-permute-start | bytes 196616 | tf_op jit(solution)/shard_map/ppermute | solution.py:18
  102.9 4.1 %collective-permute-done.9 = bf16[128,1,4,64]{0,3,2,1:T(8,128)(2,1)S(1)} collective-permute-done((bf16[128,1,4,64]{0,3,2,1:T(8,128)(2,1)S(1)}, bf16[128,1,4,64]{0,3,2,1:T(8,128)(2,1)S(1)}, u32[]{:S(2)}, u32[]{:S(2)}) %collective-permute-start.9) | collective-permute-done | bytes 65568 | tf_op jit(solution)/shard_map/ppermute | solution.py:19
  107.1 4.9 %collective-permute-start.11 = (bf16[128,4,1,64]{0,3,2,1:T(8,128)(2,1)S(1)}, bf16[128,4,1,64]{0,3,2,1:T(8,128)(2,1)S(1)}, u32[]{:S(2)}, u32[]{:S(2)}) collective-permute-start(bf16[128,4,1,64]{0,3,2,1:T(8,128)(2,1)S(1)} %get-tuple-element.23), channel_id=1, source_target_pairs={{1,0},{2,1},{3,2},{4,3},{5,4},{6,5},{7,6},{8,7},{9,8},{10,9},{11,1... | collective-permute-start | bytes 196616 | tf_op jit(solution)/shard_map/ppermute | solution.py:19
  112.0 1.9 collective-permute-start.10
  114.2 5.8 %collective-permute-done.10 = bf16[128,4,1,64]{0,3,2,1:T(8,128)(2,1)S(1)} collective-permute-done((bf16[128,4,1,64]{0,3,2,1:T(8,128)(2,1)S(1)}, bf16[128,4,1,64]{0,3,2,1:T(8,128)(2,1)S(1)}, u32[]{:S(2)}, u32[]{:S(2)}) %collective-permute-start.10) | collective-permute-done | bytes 65568 | tf_op jit(solution)/shard_map/ppermute | solution.py:18
  127.0 2.2 copy.120
  129.2 1.9 fusion.210
  140.7 3.3 copy.149
  145.6 4.6 %collective-permute-start.12 = (bf16[64,1,8,128]{3,0,2,1:T(8,128)(2,1)S(1)}, bf16[64,1,8,128]{3,0,2,1:T(8,128)(2,1)S(1)}, u32[]{:S(2)}, u32[]{:S(2)}) collective-permute-start(bf16[64,1,8,128]{3,0,2,1:T(8,128)(2,1)S(1)} %get-tuple-element.16), channel_id=1, source_target_pairs={{0,16},{16,32},{32,48},{48,64},{64,80},{80,96},{96,112},{1,17},{17... | collective-permute-start | bytes 393224 | tf_op jit(solution)/shard_map/ppermute | solution.py:18
  150.1 134.6 %all-reduce.6.cloned.1.call-done = f32[27,64,32]{1,2,0:T(8,128)} async-done(((f32[27,64,32]{1,2,0:T(8,128)}), f32[27,64,32]{1,2,0:T(8,128)}) %all-reduce.6.cloned.1.call-update) | async-done | bytes 221200 | tf_op jit(solution)/shard_map/psum | solution.py:142
  286.6 1.9 collective-permute-start.14
  288.5 6.3 %collective-permute-start.15 = (bf16[64,6,1,128]{3,0,2,1:T(8,128)(2,1)S(1)}, bf16[64,6,1,128]{3,0,2,1:T(8,128)(2,1)S(1)}, u32[]{:S(2)}, u32[]{:S(2)}) collective-permute-start(bf16[64,6,1,128]{3,0,2,1:T(8,128)(2,1)S(1)} %get-tuple-element.15), channel_id=1, source_target_pairs={{1,0},{2,1},{3,2},{4,3},{5,4},{6,5},{7,6},{8,7},{9,8},{10,9},{11,1... | collective-permute-start | bytes 294920 | tf_op jit(solution)/shard_map/ppermute | solution.py:19
  306.6 33.3 %psum.16 = bf16[27,8,64]{2,0,1:T(8,128)(2,1)S(1)} all-reduce(bf16[27,8,64]{2,0,1:T(8,128)(2,1)} %reduce-scatter.2.cloned.1.call-done), channel_id=1, replica_groups=mesh['depth'=8,'height'=16] {'depth'}, use_global_device_ids=true, to_apply=%region_2.3 | all-reduce | flops 13824 | bytes 55296 | tf_op jit(solution)/shard_map/psum | solution.py:126
  (243 shorter events, 65.6 us)
Async XLA Ops:
  8.0 18.7 %copy-start = (bf16[32,4,8,128]{3,2,1,0:T(8,128)(2,1)S(1)}, bf16[32,4,8,128]{3,2,1,0:T(8,128)(2,1)}, u32[]{:S(2)}) copy-start(bf16[32,4,8,128]{3,2,1,0:T(8,128)(2,1)} %param.4) | copy-start | bytes 786436
  8.0 18.7 %copy-start.6 = (bf16[27,64,32]{1,2,0:T(8,128)(2,1)S(1)}, bf16[27,64,32]{1,2,0:T(8,128)(2,1)}, u32[]{:S(2)}) copy-start(bf16[27,64,32]{1,2,0:T(8,128)(2,1)} %param.5) | copy-start | bytes 331780
  8.0 276.7 %all-reduce.6.cloned.1.call-start = ((), (), s32[]{:S(2)}) async-start(), calls=%async_computation.1 | async-start | bytes 884736 | tf_op jit(solution)/shard_map/psum | solution.py:142
  9.0 5.4 %collective-permute-start = (bf16[32,1,8,128]{3,0,2,1:T(8,128)(2,1)S(1)}, bf16[32,1,8,128]{3,0,2,1:T(8,128)(2,1)S(1)}, u32[]{:S(2)}, u32[]{:S(2)}) collective-permute-start(bf16[32,1,8,128]{3,0,2,1:T(8,128)(2,1)S(1)} %copy.321), channel_id=1, source_target_pairs={{0,16},{16,32},{32,48},{48,64},{64,80},{80,96},{96,112},{1,17},{17... | collective-permute-start | bytes 196616 | tf_op jit(solution)/shard_map/ppermute | solution.py:18
  12.5 6.2 %collective-permute-start.1 = (bf16[32,1,8,128]{3,0,2,1:T(8,128)(2,1)S(1)}, bf16[32,1,8,128]{3,0,2,1:T(8,128)(2,1)S(1)}, u32[]{:S(2)}, u32[]{:S(2)}) collective-permute-start(bf16[32,1,8,128]{3,0,2,1:T(8,128)(2,1)S(1)} %copy.322), channel_id=1, source_target_pairs={{16,0},{32,16},{48,32},{64,48},{80,64},{96,80},{112,96},{17,1},{33... | collective-permute-start | bytes 196616 | tf_op jit(solution)/shard_map/ppermute | solution.py:19
  15.6 19.9 %copy-start.4 = (bf16[32,5,8,128]{3,0,2,1:T(8,128)(2,1)}, bf16[32,5,8,128]{3,0,2,1:T(8,128)(2,1)S(1)}, u32[]{:S(2)}) copy-start(bf16[32,5,8,128]{3,0,2,1:T(8,128)(2,1)S(1)} %get-tuple-element.28) | copy-start | bytes 983044
  18.7 19.6 %copy-start.2 = (bf16[32,5,8,128]{3,0,2,1:T(8,128)(2,1)}, bf16[32,5,8,128]{3,0,2,1:T(8,128)(2,1)S(1)}, u32[]{:S(2)}) copy-start(bf16[32,5,8,128]{3,0,2,1:T(8,128)(2,1)S(1)} %get-tuple-element.35) | copy-start | bytes 983044
  18.8 8.3 %collective-permute-start.2 = (bf16[32,6,1,128]{3,0,2,1:T(8,128)(2,1)S(1)}, bf16[32,6,1,128]{3,0,2,1:T(8,128)(2,1)S(1)}, u32[]{:S(2)}, u32[]{:S(2)}) collective-permute-start(bf16[32,6,1,128]{3,0,2,1:T(8,128)(2,1)S(1)} %get-tuple-element.18), channel_id=1, source_target_pairs={{0,1},{1,2},{2,3},{3,4},{4,5},{5,6},{6,7},{7,8},{8,9},{9,10},{10,1... | collective-permute-start | bytes 147464 | tf_op jit(solution)/shard_map/ppermute | solution.py:18
  20.7 7.8 %collective-permute-start.3 = (bf16[32,6,1,128]{3,0,2,1:T(8,128)(2,1)S(1)}, bf16[32,6,1,128]{3,0,2,1:T(8,128)(2,1)S(1)}, u32[]{:S(2)}, u32[]{:S(2)}) collective-permute-start(bf16[32,6,1,128]{3,0,2,1:T(8,128)(2,1)S(1)} %get-tuple-element.19), channel_id=1, source_target_pairs={{1,0},{2,1},{3,2},{4,3},{5,4},{6,5},{7,6},{8,7},{9,8},{10,9},{11,1... | collective-permute-start | bytes 147464 | tf_op jit(solution)/shard_map/ppermute | solution.py:19
  27.1 9.8 %copy-start.10 = (bf16[32,6,1,128]{3,0,2,1:T(8,128)(2,1)}, bf16[32,6,1,128]{3,0,2,1:T(8,128)(2,1)S(1)}, u32[]{:S(2)}) copy-start(bf16[32,6,1,128]{3,0,2,1:T(8,128)(2,1)S(1)} %collective-permute-done.2) | copy-start | bytes 147460
  28.5 9.5 %copy-start.8 = (bf16[32,6,1,128]{3,0,2,1:T(8,128)(2,1)}, bf16[32,6,1,128]{3,0,2,1:T(8,128)(2,1)S(1)}, u32[]{:S(2)}) copy-start(bf16[32,6,1,128]{3,0,2,1:T(8,128)(2,1)S(1)} %collective-permute-done.3) | copy-start | bytes 147460
  45.6 29.6 %collective-permute-start.4 = (bf16[64,1,4,64]{0,3,2,1:T(8,128)(2,1)S(1)}, bf16[64,1,4,64]{0,3,2,1:T(8,128)(2,1)S(1)}, u32[]{:S(2)}, u32[]{:S(2)}) collective-permute-start(bf16[64,1,4,64]{0,3,2,1:T(8,128)(2,1)S(1)} %get-tuple-element.33), channel_id=1, source_target_pairs={{0,16},{16,32},{32,48},{48,64},{64,80},{80,96},{96,112},{1,17},{17... | collective-permute-start | bytes 98312 | tf_op jit(solution)/shard_map/ppermute | solution.py:18
  50.2 25.0 %collective-permute-start.5 = (bf16[64,1,4,64]{0,3,2,1:T(8,128)(2,1)S(1)}, bf16[64,1,4,64]{0,3,2,1:T(8,128)(2,1)S(1)}, u32[]{:S(2)}, u32[]{:S(2)}) collective-permute-start(bf16[64,1,4,64]{0,3,2,1:T(8,128)(2,1)S(1)} %get-tuple-element.34), channel_id=1, source_target_pairs={{16,0},{32,16},{48,32},{64,48},{80,64},{96,80},{112,96},{17,1},{33... | collective-permute-start | bytes 98312 | tf_op jit(solution)/shard_map/ppermute | solution.py:19
  75.2 8.2 %collective-permute-start.6 = (bf16[64,4,1,64]{0,3,2,1:T(8,128)(2,1)S(1)}, bf16[64,4,1,64]{0,3,2,1:T(8,128)(2,1)S(1)}, u32[]{:S(2)}, u32[]{:S(2)}) collective-permute-start(bf16[64,4,1,64]{0,3,2,1:T(8,128)(2,1)S(1)} %get-tuple-element.24), channel_id=1, source_target_pairs={{0,1},{1,2},{2,3},{3,4},{4,5},{5,6},{6,7},{7,8},{8,9},{9,10},{10,1... | collective-permute-start | bytes 98312 | tf_op jit(solution)/shard_map/ppermute | solution.py:18
  77.5 7.6 %collective-permute-start.7 = (bf16[64,4,1,64]{0,3,2,1:T(8,128)(2,1)S(1)}, bf16[64,4,1,64]{0,3,2,1:T(8,128)(2,1)S(1)}, u32[]{:S(2)}, u32[]{:S(2)}) collective-permute-start(bf16[64,4,1,64]{0,3,2,1:T(8,128)(2,1)S(1)} %get-tuple-element.25), channel_id=1, source_target_pairs={{1,0},{2,1},{3,2},{4,3},{5,4},{6,5},{7,6},{8,7},{9,8},{10,9},{11,1... | collective-permute-start | bytes 98312 | tf_op jit(solution)/shard_map/ppermute | solution.py:19
  96.6 6.4 %collective-permute-start.8 = (bf16[128,1,4,64]{0,3,2,1:T(8,128)(2,1)S(1)}, bf16[128,1,4,64]{0,3,2,1:T(8,128)(2,1)S(1)}, u32[]{:S(2)}, u32[]{:S(2)}) collective-permute-start(bf16[128,1,4,64]{0,3,2,1:T(8,128)(2,1)S(1)} %get-tuple-element.31), channel_id=1, source_target_pairs={{0,16},{16,32},{32,48},{48,64},{64,80},{80,96},{96,112},{1,17},{17... | collective-permute-start | bytes 196616 | tf_op jit(solution)/shard_map/ppermute | solution.py:18
  100.5 6.5 %collective-permute-start.9 = (bf16[128,1,4,64]{0,3,2,1:T(8,128)(2,1)S(1)}, bf16[128,1,4,64]{0,3,2,1:T(8,128)(2,1)S(1)}, u32[]{:S(2)}, u32[]{:S(2)}) collective-permute-start(bf16[128,1,4,64]{0,3,2,1:T(8,128)(2,1)S(1)} %get-tuple-element.32), channel_id=1, source_target_pairs={{16,0},{32,16},{48,32},{64,48},{80,64},{96,80},{112,96},{17,1},{33... | collective-permute-start | bytes 196616 | tf_op jit(solution)/shard_map/ppermute | solution.py:19
  107.1 7.1 %collective-permute-start.11 = (bf16[128,4,1,64]{0,3,2,1:T(8,128)(2,1)S(1)}, bf16[128,4,1,64]{0,3,2,1:T(8,128)(2,1)S(1)}, u32[]{:S(2)}, u32[]{:S(2)}) collective-permute-start(bf16[128,4,1,64]{0,3,2,1:T(8,128)(2,1)S(1)} %get-tuple-element.23), channel_id=1, source_target_pairs={{1,0},{2,1},{3,2},{4,3},{5,4},{6,5},{7,6},{8,7},{9,8},{10,9},{11,1... | collective-permute-start | bytes 196616 | tf_op jit(solution)/shard_map/ppermute | solution.py:19
  112.0 8.0 %collective-permute-start.10 = (bf16[128,4,1,64]{0,3,2,1:T(8,128)(2,1)S(1)}, bf16[128,4,1,64]{0,3,2,1:T(8,128)(2,1)S(1)}, u32[]{:S(2)}, u32[]{:S(2)}) collective-permute-start(bf16[128,4,1,64]{0,3,2,1:T(8,128)(2,1)S(1)} %get-tuple-element.22), channel_id=1, source_target_pairs={{0,1},{1,2},{2,3},{3,4},{4,5},{5,6},{6,7},{7,8},{8,9},{9,10},{10,1... | collective-permute-start | bytes 196616 | tf_op jit(solution)/shard_map/ppermute | solution.py:18
  139.8 166.8 %reduce-scatter.2.cloned.1.call-start = ((), (), s32[]{:S(2)}) async-start(), calls=%async_computation.2 | async-start | bytes 1114112 | tf_op jit(solution)/shard_map/reduce_scatter | solution.py:128
  144.3 142.3 %collective-permute-start.13 = (bf16[64,1,8,128]{3,0,2,1:T(8,128)(2,1)S(1)}, bf16[64,1,8,128]{3,0,2,1:T(8,128)(2,1)S(1)}, u32[]{:S(2)}, u32[]{:S(2)}) collective-permute-start(bf16[64,1,8,128]{3,0,2,1:T(8,128)(2,1)S(1)} %get-tuple-element.17), channel_id=1, source_target_pairs={{16,0},{32,16},{48,32},{64,48},{80,64},{96,80},{112,96},{17,1},{33... | collective-permute-start | bytes 393224 | tf_op jit(solution)/shard_map/ppermute | solution.py:19
  145.6 141.0 %collective-permute-start.12 = (bf16[64,1,8,128]{3,0,2,1:T(8,128)(2,1)S(1)}, bf16[64,1,8,128]{3,0,2,1:T(8,128)(2,1)S(1)}, u32[]{:S(2)}, u32[]{:S(2)}) collective-permute-start(bf16[64,1,8,128]{3,0,2,1:T(8,128)(2,1)S(1)} %get-tuple-element.16), channel_id=1, source_target_pairs={{0,16},{16,32},{32,48},{48,64},{64,80},{80,96},{96,112},{1,17},{17... | collective-permute-start | bytes 393224 | tf_op jit(solution)/shard_map/ppermute | solution.py:18
  286.6 8.6 %collective-permute-start.14 = (bf16[64,6,1,128]{3,0,2,1:T(8,128)(2,1)S(1)}, bf16[64,6,1,128]{3,0,2,1:T(8,128)(2,1)S(1)}, u32[]{:S(2)}, u32[]{:S(2)}) collective-permute-start(bf16[64,6,1,128]{3,0,2,1:T(8,128)(2,1)S(1)} %get-tuple-element.14), channel_id=1, source_target_pairs={{0,1},{1,2},{2,3},{3,4},{4,5},{5,6},{6,7},{7,8},{8,9},{9,10},{10,1... | collective-permute-start | bytes 294920 | tf_op jit(solution)/shard_map/ppermute | solution.py:18
  288.5 8.2 %collective-permute-start.15 = (bf16[64,6,1,128]{3,0,2,1:T(8,128)(2,1)S(1)}, bf16[64,6,1,128]{3,0,2,1:T(8,128)(2,1)S(1)}, u32[]{:S(2)}, u32[]{:S(2)}) collective-permute-start(bf16[64,6,1,128]{3,0,2,1:T(8,128)(2,1)S(1)} %get-tuple-element.15), channel_id=1, source_target_pairs={{1,0},{2,1},{3,2},{4,3},{5,4},{6,5},{7,6},{8,7},{9,8},{10,9},{11,1... | collective-permute-start | bytes 294920 | tf_op jit(solution)/shard_map/ppermute | solution.py:19
  (10 other events, 30.4 us)
Sparse Core Ops, SparseCore 0:
  139.9 144.7 all-reduce.5
Sparse Core Ops, SparseCore 1:
  144.6 66.4 reduce-scatter.1
where the time goes:
time: 349 us; the launch traced here: 348 us
  waiting for transfers between devices  154 us (44%)
  blocking collectives  57 us (16%)
  starting transfers between devices  52.8 us (15%)
  matrix products  43.6 us (12%)
  between operations  16.6 us (5%)
  local copies, waits for them, and re-layouts  14.2 us (4%)
  other arithmetic  10.1 us (3%)
    psum x1, waiting for transfers between devices, shards(): grad_three = lax.psum(partial_three, ('depth', 'height')) * scale_three  135 us
    psum x1, blocking collectives, shards(): depth_summed = lax.psum(partial_four.astype(jnp.bfloat16), 'depth')  33.3 us
    ppermute x8, starting transfers between devices, extended_2(): after = lax.ppermute(first, axis, down)  28.1 us
    ppermute x8, starting transfers between devices, extended_2(): before = lax.ppermute(last, axis, up)  24.6 us
    all_gather x1, blocking collectives, shards(): full_bank = lax.all_gather(filters_four, 'height', axis=1, tiled=True)  23.7 us
    dot_general x54, matrix products, forward_taps(): jnp.einsum('oi,idhw->odhw', weights[9 * first + 3 * second + third], wind...  16.9 us
    dot_general x54, matrix products, weight_taps(): jnp.einsum('odhw,idhw->oi', delta, window_piece, preferred_element_type=j...  14.4 us
    dot_general x54, matrix products, transpose_taps(): jnp.einsum('oi,odhw->idhw', weights[9 * first + 3 * second + third], wind...  12.3 us
  transfers between devices with their start and end apart: 18, of which 9 were waited for; matrix products, arithmetic and copies ran while one was open for 5% of the time, Pallas kernels for 0%

commit v1 on v0

--- a/solution.py
+++ b/solution.py
@@ -6,6 +6,12 @@
 
 TANH_SCALE = 0.7978845608028654
 CUBIC_TERM = 0.044715
+
+
+def summed_here(block, axis):
+    blocks = lax.all_gather(block, axis, axis=0, tiled=False)
+    summed = blocks.sum(axis=0)
+    return summed
 
 
 def extended_2(x, sides, width):
@@ -139,7 +145,7 @@
     )
     delta_three = (spread * gelu_slope(act_three)).astype(jnp.bfloat16)
     partial_three = weight_taps(delta_three, padded, depth_cells, height_cells, width_cells)
-    grad_three = lax.psum(partial_three, ("depth", "height")) * scale_three
+    grad_three = summed_here(partial_three, ("depth", "height")) * scale_three
     delta_extended = extended_2(delta_three, (("depth", 1), ("height", 2)), 1)
     grad_volume = transpose_taps(
         pad_width(delta_extended), filters_three, depth_cells, height_cells, width_cells

time: 349 us -> 487 us (1.40)
  waiting for transfers between devices: 154 us -> 272 us
  other arithmetic: 10.1 us -> 28.1 us
    all_gather x0 -> x1, waiting for transfers between devices: none -> 224 us  [summed_here(): blocks = lax.all_gather(block, axis, axis=0, tiled=False)]
    psum x1 -> x0, waiting for transfers between devices: 135 us -> none  [shards(): grad_three = lax.psum(partial_three, ('depth', 'height')) * scale_three]
    reduce_scatter x1, waiting for transfers between devices: 0.01 us -> 27.2 us  [shards(): lax.psum_scatter(depth_summed, 'height', scatter_dimension=1, tiled=True)]
    reduce_sum x0 -> x1, other arithmetic: none -> 18.1 us  [summed_here(): summed = blocks.sum(axis=0)]
  transfers between devices with their start and end apart: 18 -> 18, of which waited for: 9 -> 13; matrix products, arithmetic and copies ran while one was open for 5% -> 7% of each run, Pallas kernels for 0% -> 0%
where the time goes in v1:
time: 487 us; the launch traced here: 486 us
  waiting for transfers between devices  272 us (56%)
  blocking collectives  61.6 us (13%)
  starting transfers between devices  53 us (11%)
  matrix products  43.1 us (9%)
  other arithmetic  28.1 us (6%)
  between operations  16.6 us (3%)
  local copies, waits for them, and re-layouts  11.4 us (2%)
    all_gather x1, waiting for transfers between devices, summed_here(): blocks = lax.all_gather(block, axis, axis=0, tiled=False)  224 us
    psum x1, blocking collectives, shards(): depth_summed = lax.psum(partial_four.astype(jnp.bfloat16), 'depth')  37.7 us
    ppermute x8, starting transfers between devices, extended_2(): after = lax.ppermute(first, axis, down)  28.1 us
    reduce_scatter x1, waiting for transfers between devices, shards(): lax.psum_scatter(depth_summed, 'height', scatter_dimension=1, tiled=True)  27.2 us
    ppermute x8, starting transfers between devices, extended_2(): before = lax.ppermute(last, axis, up)  24.6 us
    all_gather x1, blocking collectives, shards(): full_bank = lax.all_gather(filters_four, 'height', axis=1, tiled=True)  23.9 us
    reduce_sum x1, other arithmetic, summed_here(): summed = blocks.sum(axis=0)  18.1 us
    dot_general x54, matrix products, forward_taps(): jnp.einsum('oi,idhw->odhw', weights[9 * first + 3 * second + third], wind...  17.1 us
  transfers between devices with their start and end apart: 18, of which 13 were waited for; matrix products, arithmetic and copies ran while one was open for 7% of the time, Pallas kernels for 0%

profile of v1, /device:TPU:6, one launch (start us, length us, event | category | flops | bytes accessed | tf_op | source)
XLA Modules:
  0.0 485.7 jit_solution(8380752418296855722)
XLA Ops:
  9.0 3.5 collective-permute-start
  15.6 3.1 collective-permute-done.1
  18.8 1.9 collective-permute-start.2
  20.7 6.0 %collective-permute-start.3 = (bf16[32,6,1,128]{3,0,2,1:T(8,128)(2,1)S(1)}, bf16[32,6,1,128]{3,0,2,1:T(8,128)(2,1)S(1)}, u32[]{:S(2)}, u32[]{:S(2)}) collective-permute-start(bf16[32,6,1,128]{3,0,2,1:T(8,128)(2,1)S(1)} %get-tuple-element.19), channel_id=1, source_target_pairs={{1,0},{2,1},{3,2},{4,3},{5,4},{6,5},{7,6},{8,7},{9,8},{10,9},{11,1... | collective-permute-start | bytes 147464 | tf_op jit(solution)/shard_map/ppermute | solution.py:25
  38.5 2.1 add_multiply_fusion
  42.4 2.4 reduce_sum.18
  45.8 4.6 collective-permute-start.4
  51.8 23.9 %all_gather.9 = bf16[27,128,64]{2,1,0:T(8,128)(2,1)S(1)} all-gather(bf16[27,8,64]{2,1,0:T(8,128)(2,1)} %param.6), channel_id=1, replica_groups=mesh['depth'=8,'height'=16] {'height'}, dimensions={1}, use_global_device_ids=true | all-gather | bytes 470016 | tf_op jit(solution)/shard_map/all_gather | solution.py:126
  75.7 2.3 collective-permute-start.6
  78.0 5.7 %collective-permute-start.7 = (bf16[64,4,1,64]{0,3,2,1:T(8,128)(2,1)S(1)}, bf16[64,4,1,64]{0,3,2,1:T(8,128)(2,1)S(1)}, u32[]{:S(2)}, u32[]{:S(2)}) collective-permute-start(bf16[64,4,1,64]{0,3,2,1:T(8,128)(2,1)S(1)} %get-tuple-element.25), channel_id=1, source_target_pairs={{1,0},{2,1},{3,2},{4,3},{5,4},{6,5},{7,6},{8,7},{9,8},{10,9},{11,1... | collective-permute-start | bytes 98312 | tf_op jit(solution)/shard_map/ppermute | solution.py:25
  97.2 4.0 collective-permute-start.8
  103.6 4.1 collective-permute-done.9
  108.4 4.9 %collective-permute-start.11 = (bf16[128,4,1,64]{0,3,2,1:T(8,128)(2,1)}, bf16[128,4,1,64]{0,3,2,1:T(8,128)(2,1)S(1)}, u32[]{:S(2)}, u32[]{:S(2)}) collective-permute-start(bf16[128,4,1,64]{0,3,2,1:T(8,128)(2,1)} %get-tuple-element.23), channel_id=1, source_target_pairs={{1,0},{2,1},{3,2},{4,3},{5,4},{6,5},{7,6},{8,7},{9,8},{10,9},{11,1... | collective-permute-start | bytes 196616 | tf_op jit(solution)/shard_map/ppermute | solution.py:25
  113.3 1.9 collective-permute-start.10
  115.4 2.5 copy.149
  118.2 3.1 collective-permute-done.10
  128.5 2.3 fusion.210
  140.7 4.6 collective-permute-start.12
  147.8 1.9 collective-permute-start.14
  149.8 6.3 %collective-permute-start.15 = (bf16[64,6,1,128]{3,0,2,1:T(8,128)(2,1)S(1)}, bf16[64,6,1,128]{3,0,2,1:T(8,128)(2,1)S(1)}, u32[]{:S(2)}, u32[]{:S(2)}) collective-permute-start(bf16[64,6,1,128]{3,0,2,1:T(8,128)(2,1)S(1)} %get-tuple-element.15), channel_id=1, source_target_pairs={{1,0},{2,1},{3,2},{4,3},{5,4},{6,5},{7,6},{8,7},{9,8},{10,9},{11,1... | collective-permute-start | bytes 294920 | tf_op jit(solution)/shard_map/ppermute | solution.py:25
  169.7 27.2 %reduce-scatter.2.cloned.1.call-done = bf16[27,8,64]{2,0,1:T(8,128)(2,1)} async-done(((bf16[27,128,64]{2,0,1:T(8,128)(2,1)}), bf16[27,8,64]{2,0,1:T(8,128)(2,1)}) %reduce-scatter.2.cloned.1.call-update) | async-done | bytes 27664 | tf_op jit(solution)/shard_map/reduce_scatter | solution.py:134
  197.0 37.7 %psum.8 = bf16[27,8,64]{2,0,1:T(8,128)(2,1)S(1)} all-reduce(bf16[27,8,64]{2,0,1:T(8,128)(2,1)} %reduce-scatter.2.cloned.1.call-done), channel_id=1, replica_groups=mesh['depth'=8,'height'=16] {'depth'}, use_global_device_ids=true, to_apply=%region_2.3 | all-reduce | flops 13824 | bytes 55296 | tf_op jit(solution)/shard_map/psum | solution.py:132
  235.4 223.9 %all-gather.3.cloned.1.call-done = f32[3456,64,32]{1,2,0:T(8,128)} async-done(((f32[27,64,32]{1,2,0:T(8,128)}), f32[3456,64,32]{1,2,0:T(8,128)}) %all-gather.3.cloned.1.call-update) | async-done | bytes 28311568 | tf_op jit(solution)/shard_map/all_gather | solution.py:12
  459.4 18.1 %reduce_sum.19 = f32[27,64,32]{1,2,0:T(8,128)S(1)} reduce(f32[128,27,64,32]{2,3,1,0:T(8,128)} %bitcast.1362, f32[]{:T(128)} %constant.15.clone.1), dimensions={0}, to_apply=%region_1.2 | reduce | flops 7022592 | bytes 28532740 | tf_op jit(solution)/shard_map/reduce_sum | solution.py:13
  (236 shorter events, 71.2 us)
Async XLA Ops:
  8.0 18.7 %copy-start = (bf16[32,4,8,128]{3,2,1,0:T(8,128)(2,1)S(1)}, bf16[32,4,8,128]{3,2,1,0:T(8,128)(2,1)}, u32[]{:S(2)}) copy-start(bf16[32,4,8,128]{3,2,1,0:T(8,128)(2,1)} %param.4) | copy-start | bytes 786436
  8.0 18.7 %copy-start.6 = (bf16[27,64,32]{1,2,0:T(8,128)(2,1)S(1)}, bf16[27,64,32]{1,2,0:T(8,128)(2,1)}, u32[]{:S(2)}) copy-start(bf16[27,64,32]{1,2,0:T(8,128)(2,1)} %param.5) | copy-start | bytes 331780
  8.0 188.9 %reduce-scatter.2.cloned.1.call-start = ((), (), s32[]{:S(2)}) async-start(), calls=%async_computation.2 | async-start | bytes 1114112 | tf_op jit(solution)/shard_map/reduce_scatter | solution.py:134
  9.0 5.4 %collective-permute-start = (bf16[32,1,8,128]{3,0,2,1:T(8,128)(2,1)S(1)}, bf16[32,1,8,128]{3,0,2,1:T(8,128)(2,1)S(1)}, u32[]{:S(2)}, u32[]{:S(2)}) collective-permute-start(bf16[32,1,8,128]{3,0,2,1:T(8,128)(2,1)S(1)} %copy.321), channel_id=1, source_target_pairs={{0,16},{16,32},{32,48},{48,64},{64,80},{80,96},{96,112},{1,17},{17... | collective-permute-start | bytes 196616 | tf_op jit(solution)/shard_map/ppermute | solution.py:24
  12.5 6.2 %collective-permute-start.1 = (bf16[32,1,8,128]{3,0,2,1:T(8,128)(2,1)S(1)}, bf16[32,1,8,128]{3,0,2,1:T(8,128)(2,1)S(1)}, u32[]{:S(2)}, u32[]{:S(2)}) collective-permute-start(bf16[32,1,8,128]{3,0,2,1:T(8,128)(2,1)S(1)} %copy.322), channel_id=1, source_target_pairs={{16,0},{32,16},{48,32},{64,48},{80,64},{96,80},{112,96},{17,1},{33... | collective-permute-start | bytes 196616 | tf_op jit(solution)/shard_map/ppermute | solution.py:25
  15.6 19.9 %copy-start.4 = (bf16[32,5,8,128]{3,0,2,1:T(8,128)(2,1)}, bf16[32,5,8,128]{3,0,2,1:T(8,128)(2,1)S(1)}, u32[]{:S(2)}) copy-start(bf16[32,5,8,128]{3,0,2,1:T(8,128)(2,1)S(1)} %get-tuple-element.28) | copy-start | bytes 983044
  18.7 19.8 %copy-start.2 = (bf16[32,5,8,128]{3,0,2,1:T(8,128)(2,1)}, bf16[32,5,8,128]{3,0,2,1:T(8,128)(2,1)S(1)}, u32[]{:S(2)}) copy-start(bf16[32,5,8,128]{3,0,2,1:T(8,128)(2,1)S(1)} %get-tuple-element.35) | copy-start | bytes 983044
  18.8 8.3 %collective-permute-start.2 = (bf16[32,6,1,128]{3,0,2,1:T(8,128)(2,1)S(1)}, bf16[32,6,1,128]{3,0,2,1:T(8,128)(2,1)S(1)}, u32[]{:S(2)}, u32[]{:S(2)}) collective-permute-start(bf16[32,6,1,128]{3,0,2,1:T(8,128)(2,1)S(1)} %get-tuple-element.18), channel_id=1, source_target_pairs={{0,1},{1,2},{2,3},{3,4},{4,5},{5,6},{6,7},{7,8},{8,9},{9,10},{10,1... | collective-permute-start | bytes 147464 | tf_op jit(solution)/shard_map/ppermute | solution.py:24
  20.7 7.8 %collective-permute-start.3 = (bf16[32,6,1,128]{3,0,2,1:T(8,128)(2,1)S(1)}, bf16[32,6,1,128]{3,0,2,1:T(8,128)(2,1)S(1)}, u32[]{:S(2)}, u32[]{:S(2)}) collective-permute-start(bf16[32,6,1,128]{3,0,2,1:T(8,128)(2,1)S(1)} %get-tuple-element.19), channel_id=1, source_target_pairs={{1,0},{2,1},{3,2},{4,3},{5,4},{6,5},{7,6},{8,7},{9,8},{10,9},{11,1... | collective-permute-start | bytes 147464 | tf_op jit(solution)/shard_map/ppermute | solution.py:25
  27.1 9.9 %copy-start.8 = (bf16[32,6,1,128]{3,0,2,1:T(8,128)(2,1)}, bf16[32,6,1,128]{3,0,2,1:T(8,128)(2,1)S(1)}, u32[]{:S(2)}) copy-start(bf16[32,6,1,128]{3,0,2,1:T(8,128)(2,1)S(1)} %collective-permute-done.2) | copy-start | bytes 147460
  45.8 29.8 %collective-permute-start.4 = (bf16[64,1,4,64]{0,3,2,1:T(8,128)(2,1)S(1)}, bf16[64,1,4,64]{0,3,2,1:T(8,128)(2,1)S(1)}, u32[]{:S(2)}, u32[]{:S(2)}) collective-permute-start(bf16[64,1,4,64]{0,3,2,1:T(8,128)(2,1)S(1)} %get-tuple-element.33), channel_id=1, source_target_pairs={{0,16},{16,32},{32,48},{48,64},{64,80},{80,96},{96,112},{1,17},{17... | collective-permute-start | bytes 98312 | tf_op jit(solution)/shard_map/ppermute | solution.py:24
  50.5 25.2 %collective-permute-start.5 = (bf16[64,1,4,64]{0,3,2,1:T(8,128)(2,1)S(1)}, bf16[64,1,4,64]{0,3,2,1:T(8,128)(2,1)S(1)}, u32[]{:S(2)}, u32[]{:S(2)}) collective-permute-start(bf16[64,1,4,64]{0,3,2,1:T(8,128)(2,1)S(1)} %get-tuple-element.34), channel_id=1, source_target_pairs={{16,0},{32,16},{48,32},{64,48},{80,64},{96,80},{112,96},{17,1},{33... | collective-permute-start | bytes 98312 | tf_op jit(solution)/shard_map/ppermute | solution.py:25
  75.7 8.2 %collective-permute-start.6 = (bf16[64,4,1,64]{0,3,2,1:T(8,128)(2,1)S(1)}, bf16[64,4,1,64]{0,3,2,1:T(8,128)(2,1)S(1)}, u32[]{:S(2)}, u32[]{:S(2)}) collective-permute-start(bf16[64,4,1,64]{0,3,2,1:T(8,128)(2,1)S(1)} %get-tuple-element.24), channel_id=1, source_target_pairs={{0,1},{1,2},{2,3},{3,4},{4,5},{5,6},{6,7},{7,8},{8,9},{9,10},{10,1... | collective-permute-start | bytes 98312 | tf_op jit(solution)/shard_map/ppermute | solution.py:24
  78.0 7.6 %collective-permute-start.7 = (bf16[64,4,1,64]{0,3,2,1:T(8,128)(2,1)S(1)}, bf16[64,4,1,64]{0,3,2,1:T(8,128)(2,1)S(1)}, u32[]{:S(2)}, u32[]{:S(2)}) collective-permute-start(bf16[64,4,1,64]{0,3,2,1:T(8,128)(2,1)S(1)} %get-tuple-element.25), channel_id=1, source_target_pairs={{1,0},{2,1},{3,2},{4,3},{5,4},{6,5},{7,6},{8,7},{9,8},{10,9},{11,1... | collective-permute-start | bytes 98312 | tf_op jit(solution)/shard_map/ppermute | solution.py:25
  97.2 6.4 %collective-permute-start.8 = (bf16[128,1,4,64]{0,3,2,1:T(8,128)(2,1)S(1)}, bf16[128,1,4,64]{0,3,2,1:T(8,128)(2,1)S(1)}, u32[]{:S(2)}, u32[]{:S(2)}) collective-permute-start(bf16[128,1,4,64]{0,3,2,1:T(8,128)(2,1)S(1)} %get-tuple-element.31), channel_id=1, source_target_pairs={{0,16},{16,32},{32,48},{48,64},{64,80},{80,96},{96,112},{1,17},{17... | collective-permute-start | bytes 196616 | tf_op jit(solution)/shard_map/ppermute | solution.py:24
  101.2 6.5 %collective-permute-start.9 = (bf16[128,1,4,64]{0,3,2,1:T(8,128)(2,1)S(1)}, bf16[128,1,4,64]{0,3,2,1:T(8,128)(2,1)S(1)}, u32[]{:S(2)}, u32[]{:S(2)}) collective-permute-start(bf16[128,1,4,64]{0,3,2,1:T(8,128)(2,1)S(1)} %get-tuple-element.32), channel_id=1, source_target_pairs={{16,0},{32,16},{48,32},{64,48},{80,64},{96,80},{112,96},{17,1},{33... | collective-permute-start | bytes 196616 | tf_op jit(solution)/shard_map/ppermute | solution.py:25
  108.4 9.8 %collective-permute-start.11 = (bf16[128,4,1,64]{0,3,2,1:T(8,128)(2,1)}, bf16[128,4,1,64]{0,3,2,1:T(8,128)(2,1)S(1)}, u32[]{:S(2)}, u32[]{:S(2)}) collective-permute-start(bf16[128,4,1,64]{0,3,2,1:T(8,128)(2,1)} %get-tuple-element.23), channel_id=1, source_target_pairs={{1,0},{2,1},{3,2},{4,3},{5,4},{6,5},{7,6},{8,7},{9,8},{10,9},{11,1... | collective-permute-start | bytes 196616 | tf_op jit(solution)/shard_map/ppermute | solution.py:25
  113.3 8.0 %collective-permute-start.10 = (bf16[128,4,1,64]{0,3,2,1:T(8,128)(2,1)S(1)}, bf16[128,4,1,64]{0,3,2,1:T(8,128)(2,1)S(1)}, u32[]{:S(2)}, u32[]{:S(2)}) collective-permute-start(bf16[128,4,1,64]{0,3,2,1:T(8,128)(2,1)S(1)} %get-tuple-element.22), channel_id=1, source_target_pairs={{0,1},{1,2},{2,3},{3,4},{4,5},{5,6},{6,7},{7,8},{8,9},{9,10},{10,1... | collective-permute-start | bytes 196616 | tf_op jit(solution)/shard_map/ppermute | solution.py:24
  117.9 341.4 %all-gather.3.cloned.1.call-start = ((), (), s32[]{:S(2)}) async-start(), calls=%async_computation.1 | async-start | bytes 57065472 | tf_op jit(solution)/shard_map/all_gather | solution.py:12
  137.7 7.6 %copy-start.7 = (bf16[27,64,32]{1,2,0:T(8,128)(2,1)S(1)}, bf16[27,64,32]{1,2,0:T(8,128)(2,1)}, u32[]{:S(2)}) copy-start(bf16[27,64,32]{1,2,0:T(8,128)(2,1)} %param.5) | copy-start | bytes 331780
  139.4 7.5 %collective-permute-start.13 = (bf16[64,1,8,128]{3,0,2,1:T(8,128)(2,1)S(1)}, bf16[64,1,8,128]{3,0,2,1:T(8,128)(2,1)S(1)}, u32[]{:S(2)}, u32[]{:S(2)}) collective-permute-start(bf16[64,1,8,128]{3,0,2,1:T(8,128)(2,1)S(1)} %get-tuple-element.17), channel_id=1, source_target_pairs={{16,0},{32,16},{48,32},{64,48},{80,64},{96,80},{112,96},{17,1},{33... | collective-permute-start | bytes 393224 | tf_op jit(solution)/shard_map/ppermute | solution.py:25
  140.7 7.1 %collective-permute-start.12 = (bf16[64,1,8,128]{3,0,2,1:T(8,128)(2,1)S(1)}, bf16[64,1,8,128]{3,0,2,1:T(8,128)(2,1)S(1)}, u32[]{:S(2)}, u32[]{:S(2)}) collective-permute-start(bf16[64,1,8,128]{3,0,2,1:T(8,128)(2,1)S(1)} %get-tuple-element.16), channel_id=1, source_target_pairs={{0,16},{16,32},{32,48},{48,64},{64,80},{80,96},{96,112},{1,17},{17... | collective-permute-start | bytes 393224 | tf_op jit(solution)/shard_map/ppermute | solution.py:24
  147.8 10.4 %collective-permute-start.14 = (bf16[64,6,1,128]{3,0,2,1:T(8,128)(2,1)S(1)}, bf16[64,6,1,128]{3,0,2,1:T(8,128)(2,1)S(1)}, u32[]{:S(2)}, u32[]{:S(2)}) collective-permute-start(bf16[64,6,1,128]{3,0,2,1:T(8,128)(2,1)S(1)} %get-tuple-element.14), channel_id=1, source_target_pairs={{0,1},{1,2},{2,3},{3,4},{4,5},{5,6},{6,7},{7,8},{8,9},{9,10},{10,1... | collective-permute-start | bytes 294920 | tf_op jit(solution)/shard_map/ppermute | solution.py:24
  149.8 10.2 %collective-permute-start.15 = (bf16[64,6,1,128]{3,0,2,1:T(8,128)(2,1)S(1)}, bf16[64,6,1,128]{3,0,2,1:T(8,128)(2,1)S(1)}, u32[]{:S(2)}, u32[]{:S(2)}) collective-permute-start(bf16[64,6,1,128]{3,0,2,1:T(8,128)(2,1)S(1)} %get-tuple-element.15), channel_id=1, source_target_pairs={{1,0},{2,1},{3,2},{4,3},{5,4},{6,5},{7,6},{8,7},{9,8},{10,9},{11,1... | collective-permute-start | bytes 294920 | tf_op jit(solution)/shard_map/ppermute | solution.py:25
  (6 other events, 8.3 us)
Sparse Core Ops, SparseCore 0:
  118.1 78.8 reduce-scatter.1
Sparse Core Ops, SparseCore 1:
  139.5 319.8 all-gather.2
